TPU v7x, 32 devices: a whole 2x2x4 slice. The times are simulated.
32 devices in a mesh: grp: 4 (over y, x), dp: 2 (over core), tp: 4 (over z).
Axes of the slice: x: 2, y: 2, z: 4, core: 2. Of those that a mesh axis runs over, the one named last changes fastest.
Arguments:
- inputs: bfloat16 [16384, 640], P(('grp', 'dp', 'tp')), may hold values from -6 to 6
- memory: bfloat16 [3, 16384, 640], P(None, ('grp', 'dp', 'tp')), may hold values from -6 to 6
- out_grad: bfloat16 [16384, 640], P(('grp', 'dp', 'tp')), may hold values from -6 to 6
- lengths: int32 [64], P(('grp', 'dp')), may hold values from 33 to 256
- src_lengths: int32 [64], P(('grp', 'dp')), may hold values from 33 to 256
- configs: int32 [4, 4], P('grp'), may hold values from 1 to 3072, as said below
- norm_gain: float32 [3, 640], replicated, may hold values from 0.5 to 1.5
- norm_bias: float32 [3, 640], replicated, may hold values from -3 to 3
- self_qkv: bfloat16 [640, 3, 640], P(None, None, 'tp'), may hold values from -0.25 to 0.25
- self_out: bfloat16 [640, 640], P('tp'), may hold values from -1 to 1
- cross_q: bfloat16 [640, 640], P(None, 'tp'), may hold values from -0.25 to 0.25
- cross_kv: bfloat16 [640, 2, 640], P(None, None, 'tp'), may hold values from -0.25 to 0.25
- cross_out: bfloat16 [640, 640], P('tp'), may hold values from -1 to 1
- ffn_in: bfloat16 [640, 3072], P(None, 'tp'), may hold values from -0.25 to 0.25
- ffn_in_bias: float32 [3072], P('tp'), may hold values from -3 to 3
- ffn_out: bfloat16 [3072, 640], P('tp'), may hold values from -0.21875 to 0.21875
- ffn_out_bias: float32 [640], replicated, may hold values from -3 to 3
Outputs:
- layer_out: float32 [16384, 640], P(('grp', 'dp', 'tp'))
- input_grad: float32 [16384, 640], P(('grp', 'dp', 'tp'))
- memory_grad: float32 [3, 16384, 640], P(None, ('grp', 'dp', 'tp'))
- norm_gain_grad: float32 [3, 640], replicated
- norm_bias_grad: float32 [3, 640], replicated
- self_qkv_grad: float32 [640, 3, 640], P(None, None, 'tp')
- self_out_grad: float32 [640, 640], P('tp')
- cross_q_grad: float32 [640, 640], P(None, 'tp')
- cross_kv_grad: float32 [640, 2, 640], P(None, None, 'tp')
- cross_out_grad: float32 [640, 640], P('tp')
- ffn_in_grad: float32 [640, 3072], P(None, 'tp')
- ffn_in_bias_grad: float32 [3072], P('tp')
- ffn_out_grad: float32 [3072, 640], P('tp')
- ffn_out_bias_grad: float32 [640], replicated
Inputs may be any that keep to these rules, and one draw needn't show every extreme that they name: Row g of configs is group g's sub-net: width 4 * 128 or 640; heads 8 // 2 or 8; hidden units 3072 // 3, 2048 or 3072; encoder layers averaged 1 to 3. Some group has 3072 hidden units and some group averages one layer.
All inputs are finite; a program needn't handle non-finite values.
Results may differ from a plain program's by a relative error of at most 0.017.
Values may be sent and summed in bfloat16 or wider, within the bound.
A program may use at most 128 MiB of HBM per device.

v0:
```python
import functools
import types

import jax
import jax.numpy as jnp
from jax import lax
from jax.experimental import pallas as pl
from jax.experimental.pallas import tpu as pltpu
from jax.sharding import PartitionSpec as P

HD = 80
LEN = 256
EPSILON = 1e-05
NEGATIVE = -1e30
SCALE = HD ** (-0.5)
LOG2E = 1.4426950408889634
F32 = jnp.float32
BF16 = jnp.bfloat16


MESH = pl.DeviceIdType.MESH


class Place:
    def __init__(self):
        self.tps = lax.axis_size("tp")
        self.extra = lax.axis_size("dp") // 2
        assert lax.axis_size("grp") == 4 and lax.axis_size("dp") % 2 == 0
        grp, dp, tp = (lax.axis_index(name) for name in ("grp", "dp", "tp"))
        core, low, high = dp % 2, grp % 2, grp // 2
        flip_low, flip_high = grp + 1 - 2 * low, grp + 2 - 4 * high
        self.grp, self.dp, self.tp, self.core = grp, dp, tp, core
        self.first_bit = (1 - core) * low + core * high
        self.second_bit = (1 - core) * high + core * low
        self.first = ((1 - core) * flip_low + core * flip_high, dp, tp)
        self.second = ((1 - core) * flip_high + core * flip_low, dp, tp)
        self.across = (3 - grp, dp, tp)
        self.sibling = (grp, dp + 1 - 2 * core, tp)
        self.above = (grp, dp, tp + 1)
        self.below = (grp, dp, tp - 1)
        self.has_above = tp < self.tps - 1
        self.has_below = tp > 0

    def copy_of(self, step):
        return (self.grp, ((self.dp // 2 + step) % self.extra) * 2 + self.core, self.tp)

    def nth_block(self, k):
        size = self.tps
        upper = (2 * self.tp) // size
        lead = (1 - upper) * self.tp + upper * (size - 1 - self.tp)
        spot = k + (k + size - lead) // size
        return (1 - upper) * spot + upper * (size - 1 - spot)

    def along(self, tp):
        return (self.grp, self.dp, tp)

    def barrier(self):
        sem = pltpu.get_barrier_semaphore()
        partners = [self.first, self.second, self.across, self.sibling]
        partners += [self.along((self.tp + step) % self.tps) for step in range(1, self.tps)]
        partners += [self.copy_of(step) for step in range(1, self.extra)]
        for device in partners:
            pl.semaphore_signal(sem, inc=1, device_id=device, device_id_type=MESH)
        pl.semaphore_wait(sem, len(partners))


def push(src, dst, send_sem, recv_sem, device):
    return pltpu.make_async_remote_copy(
        src_ref=src, dst_ref=dst, send_sem=send_sem, recv_sem=recv_sem, device_id=device, device_id_type=MESH
    )


def rows_of(ref, lead, start, count):
    return ref.at[lead, pl.ds(pl.multiple_of(start, 16), count)]


def add_units(total, term, unit):
    def step(i, carry):
        rows = pl.ds(pl.multiple_of(i * unit, 16), unit)
        total[rows] = total[rows] + term[rows]
        return carry

    lax.fori_loop(0, total.shape[0] // unit, step, 0)


class Spread:
    KINDS = 6

    def __init__(self, place, view, unit, sems):
        self.place, self.view, self.unit, self.sems = place, view, unit, sems
        f, s, c = place.first_bit, place.second_bit, place.core
        self.table = (
            (place.second, c * 4 + f * 2 + s, c * 4 + f * 2 + 1 - s, 1),
            (place.first, c * 4 + f * 2, c * 4 + 2 - f * 2, 2),
            (place.sibling, c * 4, 4 - c * 4, 4),
        )

    def region(self, start, count):
        return self.view(start * self.unit, count * self.unit)

    def own(self):
        return self.region(self.table[0][1], 1)

    def copy(self, n, lands=False):
        device, leaves, landing, count = self.table[n]
        part = self.region(landing if lands else leaves, count)
        return push(part, part, self.sems(2 * n), self.sems(2 * n + 1), device)

    def step(self, stage):
        if stage > 0:
            self.copy(stage - 1, lands=True).wait_recv()
        if stage < 3:
            self.copy(stage).start()

    def finish(self):
        for n in range(3):
            self.copy(n).wait_send()


class Gather:
    KINDS = Spread.KINDS + 3

    def __init__(self, place, buffers, sems):
        self.place, self.buffers, self.sems = place, buffers, sems
        self.unit = [ref.shape[1] // 8 for ref in buffers]
        self.others = place.tps - 1

    def spread(self, g, j):
        return Spread(
            self.place,
            lambda start, count: rows_of(self.buffers[g], j, start, count),
            self.unit[g],
            lambda kind: self.sems.at[kind, g, j],
        )

    def relays(self, g, j):
        p = self.place
        part = self.spread(g, j).own()
        sem = lambda n: self.sems.at[Spread.KINDS + n, g, j]
        return (
            (jnp.logical_and(j <= p.tp, p.has_above), push(part, part, sem(0), sem(2), p.above)),
            (jnp.logical_and(j >= p.tp, p.has_below), push(part, part, sem(1), sem(2), p.below)),
        )

    def start(self, g):
        for needed, copy in self.relays(g, self.place.tp):
            pl.when(needed)(copy.start)

    def step(self, g, k, stage):
        j = self.place.nth_block(k)
        if stage == 0:
            relays = self.relays(g, j)
            relays[0][1].wait_recv()
            for needed, copy in relays:
                pl.when(needed)(copy.start)
        self.spread(g, j).step(stage)

    def drain(self, g, j):
        for needed, copy in self.relays(g, j):
            pl.when(needed)(copy.wait_send)

        @pl.when(j != self.place.tp)
        def _():
            self.spread(g, j).finish()


class Line:
    def __init__(self, place, buffer, sems):
        self.place, self.buffer, self.sems = place, buffer, sems

    def relays(self, j):
        p = self.place
        part = self.buffer.at[j]
        return (
            (jnp.logical_and(j <= p.tp, p.has_above), push(part, part, self.sems.at[0, j], self.sems.at[2, j], p.above)),
            (jnp.logical_and(j >= p.tp, p.has_below), push(part, part, self.sems.at[1, j], self.sems.at[2, j], p.below)),
        )

    def start(self):
        for needed, copy in self.relays(self.place.tp):
            pl.when(needed)(copy.start)

    def step(self, k):
        j = self.place.nth_block(k)
        relays = self.relays(j)
        relays[0][1].wait_recv()
        for needed, copy in relays:
            pl.when(needed)(copy.start)

    def finish(self):
        for j in range(self.place.tps):
            for needed, copy in self.relays(j):
                pl.when(needed)(copy.wait_send)


class Reduce:
    KINDS = 8 + Spread.KINDS + 2

    def __init__(self, place, grads, halves, planes, lines, extras, totals, sems):
        self.place, self.grads, self.totals, self.sems = place, grads, totals, sems
        self.halves, self.planes, self.lines, self.extras = halves, planes, lines, extras
        self.unit = [ref.shape[1] // 8 for ref in grads]

    def sem(self, kind, g, j):
        return self.sems.at[kind, g, j]

    def rows(self, g, j, half, unit, count=1):
        size = self.unit[g]
        return rows_of(self.grads[g], j, (half * 4 + unit) * size, count * size)

    def move(self, g, j, stage):
        p, size = self.place, self.unit[g]
        if stage == 0:
            part, landing, device = self.rows(g, j, 1 - p.core, 0, 4), self.halves[g].at[j], p.sibling
        elif stage == 1:
            part, device = self.rows(g, j, p.core, 2 - p.first_bit * 2, 2), p.first
            landing = self.planes[g].at[j, pl.ds(0, 2 * size)]
        else:
            part, device = self.rows(g, j, p.core, p.first_bit * 2 + 1 - p.second_bit), p.second
            landing = self.planes[g].at[j, pl.ds(2 * size, size)]
        return push(part, landing, self.sem(2 * stage, g, j), self.sem(2 * stage + 1, g, j), device)

    def kept(self, g, j, stage):
        p, size = self.place, self.unit[g]
        if stage == 0:
            return self.rows(g, j, p.core, 0, 4), self.halves[g].at[j]
        if stage == 1:
            return self.rows(g, j, p.core, p.first_bit * 2, 2), self.planes[g].at[j, pl.ds(0, 2 * size)]
        return self.piece(g, j), self.planes[g].at[j, pl.ds(2 * size, size)]

    def piece(self, g, j):
        p = self.place
        return self.rows(g, j, p.core, p.first_bit * 2 + p.second_bit)

    def along(self, g, j):
        p = self.place
        return push(self.piece(g, j), self.lines[g].at[p.tp], self.sem(6, g, j), self.sem(7, g, p.tp), p.along(j))

    def from_place(self, g, j):
        p = self.place
        return push(self.piece(g, j), self.lines[g].at[j], self.sem(6, g, j), self.sem(7, g, j), p.along(j))

    def step(self, g, j, stage):
        if stage > 0:
            self.move(g, j, stage - 1).wait_recv()
            add_units(*self.kept(g, j, stage - 1), self.unit[g])
        if stage < 3:
            self.move(g, j, stage).start()
        else:
            pl.when(j != self.place.tp)(self.along(g, j).start)

    def spread(self, g):
        return Spread(
            self.place,
            lambda start, count: self.totals[g].at[pl.ds(pl.multiple_of(start, 16), count)],
            self.unit[g],
            lambda kind: self.sems.at[8 + kind, g, 0],
        )

    def copies(self, g, step):
        p = self.place
        base = self.KINDS - 2
        return push(
            self.piece(g, p.tp), self.extras[g].at[step], self.sem(base, g, step), self.sem(base + 1, g, step), p.copy_of(step)
        )

    def settle(self, g):
        p = self.place
        piece = self.piece(g, p.tp)
        total = piece[...].astype(F32)
        for k in range(p.tps - 1):
            j = p.nth_block(k)
            self.from_place(g, j).wait_recv()
            total = total + self.lines[g][j].astype(F32)
        if p.extra > 1:
            piece[...] = total.astype(BF16)
            for step in range(1, p.extra):
                self.copies(g, step).start()
            for step in range(1, p.extra):
                self.copies(g, step).wait()
                total = total + self.extras[g][step].astype(F32)
        own = self.spread(g).own()
        own[...] = total.astype(BF16)
        self.spread(g).step(0)

    def share(self, g, stage):
        self.spread(g).step(stage)

    def finish(self, g):
        p = self.place
        for j in range(p.tps):
            for stage in range(3):
                self.move(g, j, stage).wait_send()
            pl.when(j != p.tp)(self.along(g, j).wait_send)
        self.spread(g).finish()


class SumSmall:
    @staticmethod
    def slots(tps, extra):
        return 8 + tps + extra

    def __init__(self, place, slots, sems):
        self.place, self.slots_ref, self.sems = place, slots, sems

    def move(self, source, target, device, kind):
        slots = self.slots_ref
        return push(slots.at[source], slots.at[target], self.sems.at[0, kind], self.sems.at[1, target], device)

    def in_plane(self):
        p = self.place
        return [self.move(2, 3 + i, device, 3 + i) for i, device in enumerate((p.second, p.first, p.across))]

    def copies(self):
        p = self.place
        return [self.move(6, 8 + p.tps + s, p.copy_of(s), 8 + p.tps + s) for s in range(1, p.extra)]

    def along(self, k, lands=False):
        p = self.place
        j = p.nth_block(k)
        return self.move(7, 8 + (j if lands else p.tp), p.along(j), 8 + j)

    def start(self):
        self.move(0, 1, self.place.sibling, 1).start()

    def exchange(self, stage):
        p, slots = self.place, self.slots_ref
        if stage == 0:
            self.move(0, 1, p.sibling, 1).wait_recv()
            slots[2] = slots[0] + slots[1]
            for copy in self.in_plane():
                copy.start()
        else:
            for copy in self.in_plane():
                copy.wait_recv()
            slots[6] = (slots[2] + slots[3]) + (slots[4] + slots[5])
            for copy in self.copies():
                copy.start()
            total = slots[6]
            for s, copy in enumerate(self.copies()):
                copy.wait_recv()
                total = total + slots[9 + p.tps + s]
            slots[7] = total
            for k in range(p.tps - 1):
                self.along(k).start()

    def total(self):
        p, slots = self.place, self.slots_ref
        value = slots[7]
        for k in range(p.tps - 1):
            self.along(k, lands=True).wait_recv()
            value = value + slots[8 + p.nth_block(k)]
        return value

    def finish(self):
        p = self.place
        self.move(0, 1, p.sibling, 1).wait_send()
        for copy in self.in_plane() + self.copies():
            copy.wait_send()
        for k in range(p.tps - 1):
            self.along(k).wait_send()


def dot_nn(left, right):
    return lax.dot_general(left, right, (((1,), (0,)), ((), ())), preferred_element_type=F32)


def dot_nt(left, right):
    return lax.dot_general(left, right, (((1,), (1,)), ((), ())), preferred_element_type=F32)


def dot_tn(left, right):
    return lax.dot_general(left, right, (((0,), (0,)), ((), ())), preferred_element_type=F32)


def column(axis, shape):
    return lax.broadcasted_iota(jnp.int32, shape, axis)


def each(count, step):

    def run(i, carry):
        step(i)
        return carry

    lax.fori_loop(0, count, run, 0)


CHUNK = 128
CUBE = 0.044715
ROOT = 0.7978845608028654


def layer_kernel(r):
    r.a2, r.a3, r.e = (r.memory.at[i] for i in range(3))
    columns = pl.ds(0, r.x.shape[1])
    r.dh, r.dm = r.before.at[:, columns], r.down.at[:, columns]
    place = Place()
    n = place.tps
    x, model = r.x, r.x.shape[1]
    owned = x.shape[0]
    sentences = owned // LEN
    local = r.c[0].shape[1]
    heads_here = local // HD
    units = r.hidden.shape[1]
    layers = r.memory.shape[0]
    weights = r.w
    lengths, sources, configs = r.lengths, r.src_lengths, r.configs
    width, heads, hidden_units, depth = (configs[0, i] for i in range(4))
    inv_width = 1.0 / jnp.full((1, 1), width.astype(F32))
    inv_depth = 1.0 / jnp.full((1, 1), depth.astype(F32))
    width_mask = (column(1, (1, model)) < width).astype(F32)

    local_sem = r.local_sems
    spots = (
        (0, 0, 3 * local), (0, 3 * local, local),
        (1, 0, local), (1, local, 2 * local), (1, 3 * local, local),
        (2, 0, weights[2].shape[1]), (3, 0, weights[3].shape[1]),
    )
    fills = [
        (g, pltpu.make_async_copy(r.shards[i], weights[g].at[place.tp, pl.ds(start, size)], local_sem.at[i]))
        for i, (g, start, size) in enumerate(spots)
    ]
    loads = [
        pltpu.make_async_copy(source, target, local_sem.at[7 + i])
        for i, (source, target) in enumerate(((r.x_in, r.x), (r.memory_in, r.memory), (r.upstream_in, r.upstream)))
    ]
    for _, copy in fills[:2]:
        copy.start()
    loads[0].start()
    for _, copy in fills[2:]:
        copy.start()
    loads[1].start()
    loads[2].start()
    r.bias[place.tp] = jnp.broadcast_to(r.bias_in[...].reshape(1, units), r.bias.shape[1:])
    place.barrier()

    gather = Gather(place, weights, r.gather_sems)
    bias = Line(place, r.bias, r.bias_sems)
    for g in range(4):
        for group, copy in fills:
            if group == g:
                copy.wait()
        gather.start(g)
        if g == 0:
            bias.start()
    order = [(g, k) for g in (0, 1) for k in range(n - 1)] + [(g, k) for k in range(n - 1) for g in (2, 3)]

    def g_tick(tick):
        for stage in range(4):
            if 0 <= tick - stage < len(order):
                gather.step(*order[tick - stage], stage)

    def block(k):
        later = (k + n - 1) // n
        return (1 - later) * place.tp + later * place.nth_block(k - 1)

    def block_last(k):
        own = k // (n - 1)
        return own * place.tp + (1 - own) * place.nth_block(k)

    def hooks(table, k, b):
        for (kk, bb), steps in table.items():

            @pl.when(jnp.logical_and(k == kk, b == bb))
            def _():
                for step in steps:
                    step()

    def chunk(i):
        return pl.ds(pl.multiple_of(i * CHUNK, CHUNK), CHUNK)

    def keep_of(i):
        per = LEN // CHUNK
        spot = column(0, (CHUNK, 1)) + (i % per) * CHUNK
        return (spot < lengths[place.tp * sentences + i // per]).astype(F32) * width_mask

    def norm_parts(rows):
        mean = jnp.sum(rows * width_mask, axis=-1, keepdims=True) * inv_width
        centred = (rows - mean) * width_mask
        spread = jnp.sum(centred * centred, axis=-1, keepdims=True) * inv_width
        rstd = lax.rsqrt(spread + EPSILON)
        return centred * rstd, rstd

    def norm(rows, which):
        hat, _ = norm_parts(rows)
        return ((hat * r.gains[which:which + 1] + r.shifts[which:which + 1]) * width_mask).astype(BF16)

    def fold(values):
        return jnp.sum(values.reshape(values.shape[0] // 8, 8, values.shape[1]), axis=0)

    def norm_backward(rows, which, upstream):
        hat, rstd = norm_parts(rows)
        upstream = upstream * width_mask
        sums = r.norm_sums
        sums[which] = sums[which] + fold(upstream * hat)
        sums[3 + which] = sums[3 + which] + fold(upstream)
        scaled = upstream * r.gains[which:which + 1]
        first = jnp.sum(scaled, axis=-1, keepdims=True) * inv_width
        second = jnp.sum(scaled * hat, axis=-1, keepdims=True) * inv_width
        return (rstd * (scaled - first - hat * second)) * width_mask

    chunks = owned // CHUNK

    def each_chunk(step):
        each(chunks, step)

    acc, da, dh = r.acc, r.da, r.dh
    zeros = jnp.zeros((CHUNK, model), F32)
    r.norm_sums[...] = jnp.zeros(r.norm_sums.shape, F32)
    r.bias_sums[...] = jnp.zeros(r.bias_sums.shape, F32)

    def sentence(b):
        return pl.ds(pl.multiple_of(b * LEN, LEN), LEN)

    def head_keep(j, h):
        return jnp.where(j * heads_here + h < heads, 1.0, 0.0).astype(F32)

    def causal(b, start, size):
        return column(0, (size, 128)) <= column(1, (size, 128)) + start

    def crossing(b, start, size):
        return column(0, (size, 1)) < sources[place.tp * sentences + b]

    def reach(g, start):
        return start + 128 if g == 0 else LEN

    def bands(h):
        return [pl.ds(i * local + h * HD, HD) for i in range(3)]

    def lanes(b):
        return pl.ds(b * LEN, LEN)

    pairs = [(b, h) for b in range(sentences) for h in range(heads_here)]

    quarters = [(i, b, h, start) for i, (b, h) in enumerate(pairs) for start in range(0, LEN, 128)]

    def attend(k, table, g, allowed):
        w, t, c, p = weights[g], r.t[g], r.c[g], r.p[g]
        j = block(k)
        hooks(table, k, 0)
        if g == 0:
            t[j] = dot_nt(w[j, :3 * local], r.a1[...]).astype(BF16)
        else:
            t[j, :local] = dot_nt(w[j, :local], r.a2[...]).astype(BF16)
            t[j, local:] = dot_nt(w[j, local:3 * local], r.m[...]).astype(BF16)
        heads_of = [[t[j, band, lanes(b)] for band in bands(h)] for b, h in pairs]
        for i, (query, keys, _) in enumerate(heads_of):
            r.scores[i] = dot_tn(keys, query)
        for i, b, h, start in quarters:
            part, size = pl.ds(start, 128), reach(g, start)
            score = jnp.where(allowed(b, start, size), r.scores[i, :size, part], NEGATIVE)
            raised = jnp.exp2((score - jnp.max(score, axis=0, keepdims=True)) * (SCALE * LOG2E))
            p[j, i, :size, part] = (raised * (1.0 / jnp.sum(raised, axis=0, keepdims=True))).astype(BF16)
            if size < LEN:
                p[j, i, size:, part] = jnp.zeros((LEN - size, 128), BF16)
        for i, (b, h) in enumerate(pairs):
            c[j, pl.ds(h * HD, HD), lanes(b)] = (dot_nn(heads_of[i][2], p[j, i]) * head_keep(j, h)).astype(BF16)
        hooks(table, k, 1)
        acc[...] = acc[...] + dot_tn(c[j], w[j, 3 * local:])

    def attend_backward(k, table, g, query_rows, key_rows):
        w, t, c, p = weights[g], r.t[g], r.c[g], r.p[g]
        j = block_last(k)
        e, dt, dc = r.e, r.dt, r.dc
        dc_all = dot_nt(w[j, 3 * local:], e[...])
        for h in range(heads_here):
            dc[h * HD:(h + 1) * HD] = (dc_all[h * HD:(h + 1) * HD] * head_keep(j, h)).astype(BF16)
        heads_of = [[t[j, band, lanes(b)] for band in bands(h)] for b, h in pairs]
        dc_of = [dc[h * HD:(h + 1) * HD, lanes(b)] for b, h in pairs]
        for i, (_, _, values) in enumerate(heads_of):
            r.scores[i] = dot_tn(values, dc_of[i])
        for i, b, h, start in quarters:
            part, size = pl.ds(start, 128), reach(g, start)
            dp, wide = r.scores[i, :size, part], p[j, i, :size, part].astype(F32)
            r.ds[i, :size, part] = (wide * (dp - jnp.sum(dp * wide, axis=0, keepdims=True))).astype(BF16)
            if size < LEN:
                r.ds[i, size:, part] = jnp.zeros((LEN - size, 128), BF16)
        for i, (b, h) in enumerate(pairs):
            (query, keys, _), (dq, dk, dv) = heads_of[i], bands(h)
            dt[dv, lanes(b)] = dot_nt(dc_of[i], p[j, i]).astype(BF16)
            dt[dq, lanes(b)] = (dot_nn(keys, r.ds[i]) * SCALE).astype(BF16)
            dt[dk, lanes(b)] = (dot_nt(query, r.ds[i]) * SCALE).astype(BF16)
        hooks(table, k, 1)
        gather.drain(g, j)
        if g == 0:
            da[...] = da[...] + dot_tn(dt[...], w[j, :3 * local])
            w[j, :3 * local] = dot_nn(dt[...], query_rows[...]).astype(BF16)
        else:
            da[...] = da[...] + dot_tn(dt[:local], w[j, :local])
            r.dm[...] = r.dm[...] + dot_tn(dt[local:], w[j, local:3 * local])
            w[j, :local] = dot_nn(dt[:local], query_rows[...]).astype(BF16)
            w[j, local:3 * local] = dot_nn(dt[local:], key_rows[...]).astype(BF16)
        w[j, 3 * local:] = dot_nn(c[j], e[...]).astype(BF16)

    def feed(k, table):
        j = block(k)
        w_up, w_down = weights[2], weights[3]
        hooks(table, k, 0)
        r.before[...] = dot_nn(r.a3[...], w_up[j]) + r.bias[j, 0:1]
        r.down[...] = dot_nt(r.e[...], w_down[j])
        step_lanes = units // 2

        def bend(i):
            for start in range(0, units, step_lanes):
                part = pl.ds(start, step_lanes)
                unit = column(1, (1, step_lanes)) + (j * units + start)
                kept = jnp.where(unit < hidden_units, 0.5, 0.0)
                sums = r.bias_sums[j, :, part]
                for line in range(4):
                    rows = pl.ds(pl.multiple_of(i * 64, 64) + line * 16, 16)
                    before = r.before[rows, part]
                    square = before * before
                    bent = jnp.tanh(before * (ROOT + ROOT * CUBE * square))
                    half = kept + kept * bent
                    through = before * half
                    r.hidden[rows, part] = through.astype(BF16)
                    slope = half + (through - through * bent) * (ROOT + 3.0 * CUBE * ROOT * square)
                    du = (r.down[rows, part] * slope).astype(BF16)
                    r.dhidden[rows, part] = du
                    sums = sums + fold(du.astype(F32))
                r.bias_sums[j, :, part] = sums

        each(owned // 64, bend)
        hooks(table, k, 1)
        acc[...] = acc[...] + dot_nn(r.hidden[...], w_down[j])
        da[...] = da[...] + dot_nt(r.dhidden[...], w_up[j])
        gather.drain(2, j)
        gather.drain(3, j)
        w_down[j] = dot_tn(r.hidden[...], r.e[...]).astype(BF16)
        w_up[j] = dot_nn(r.a3t[...], r.dhidden[...]).astype(BF16)

    loads[0].wait()

    def begin(i):
        rows = chunk(i)
        r.a1[rows] = norm(x[rows].astype(F32), 0)
        acc[rows] = zeros
        da[rows] = zeros

    each_chunk(begin)
    g_tick(0)
    loads[1].wait()

    def mix(i):
        rows = chunk(i)
        total = jnp.zeros((CHUNK, model), F32)
        for level in range(layers):
            chosen = (jnp.full((1, 1), depth) >= layers - level).astype(F32)
            total = total + chosen * r.memory[level, rows].astype(F32)
        r.m[rows] = (total * inv_depth * width_mask).astype(BF16)

    each_chunk(mix)
    g_tick(1)
    loads[2].wait()
    r.out_sums[...] = jnp.zeros(r.out_sums.shape, F32)

    def grad_in(i):
        rows = chunk(i)
        masked = r.upstream[rows].astype(F32) * keep_of(i)
        r.out_sums[...] = r.out_sums[...] + fold(masked)
        r.e[rows] = masked.astype(BF16)

    each_chunk(grad_in)
    g_tick(2)

    def ticks(*numbers):
        return [functools.partial(g_tick, i) for i in numbers]

    others = n - 1
    assert n == 4
    table = {
        (0, 1): ticks(3),
        (1, 0): ticks(4) + [functools.partial(bias.step, 0)],
        (1, 1): ticks(5),
        (2, 0): [functools.partial(bias.step, 1)],
        (2, 1): ticks(6),
        (3, 0): [functools.partial(bias.step, 2)],
        (3, 1): ticks(7),
    }
    each(n, lambda k: attend(k, table, 0, causal))

    def after_self(i):
        rows = chunk(i)
        h = x[rows].astype(F32) + acc[rows] * keep_of(i)
        r.h1[rows] = h
        r.a2[rows] = norm(h, 1)
        acc[rows] = zeros

    each_chunk(after_self)
    table2 = {(0, 0): ticks(8), (0, 1): ticks(9), (1, 1): ticks(10), (2, 1): ticks(11), (3, 1): ticks(12)}
    each(n, lambda k: attend(k, table2, 1, crossing))

    def after_cross(i):
        rows = chunk(i)
        h = r.h1[rows] + acc[rows] * keep_of(i)
        r.h2[rows] = h
        r.a3[rows] = norm(h, 2)
        acc[rows] = zeros

    each_chunk(after_cross)
    r.a3t[...] = r.a3[...].T

    reduce = Reduce(
        place, weights, r.half, r.plane, r.line, r.extra, r.total, r.reduce_sems
    )
    plan = {}

    def add(tick, order, step, *args):
        plan.setdefault(tick, []).append((order, len(plan.get(tick, ())), functools.partial(step, *args)))

    def r_tick(tick):
        for _, _, step in sorted(plan.get(tick, ()), key=lambda entry: entry[:2]):
            step()

    def store(g):
        return pltpu.make_async_copy(r.total[g], r.blocks[g], local_sem.at[10 + g])

    times = {
        3: ([(1, 2, 6, 10), (3, 4, 8, 11), (5, 6, 9, 13), (7, 9, 11, 15)], (17, 19, 21, 23)),
        2: ([(1, 3, 6, 9), (3, 6, 8, 11), (5, 8, 10, 13), (7, 9, 12, 16)], (18, 20, 22, 24)),
        1: ([(10, 11, 14, 16), (12, 14, 16, 18), (14, 15, 19, 21), (16, 17, 19, 21)], (23, 25, 27, 29)),
        0: ([(19, 20, 22, 24), (21, 22, 24, 25), (23, 24, 25, 26), (25, 26, 27, 28)], (28, 29, 30, 31)),
    }
    for late, g in enumerate((3, 2, 1, 0)):
        for k, stages in enumerate(times[g][0]):
            j = block(k) if g > 1 else block_last(k)
            for stage, tick in enumerate(stages):
                add(tick, stage, reduce.step, g, j, stage)
        for stage, tick in enumerate(times[g][1]):
            if stage == 0:
                add(tick, 20 - late, reduce.settle, g)
            else:
                add(tick, 30 + stage - late, reduce.share, g, stage)
        add(times[g][1][-1], 50, lambda g=g: store(g).start())

    def reduce_ticks(*numbers):
        return [functools.partial(r_tick, i) for i in numbers]

    def at_end(k, numbers):
        for kk, number in enumerate(numbers):

            @pl.when(k == kk)
            def _():
                r_tick(number)

    table3 = {(0, 0): ticks(13), (0, 1): ticks(14), (1, 1): reduce_ticks(2), (2, 1): reduce_ticks(4), (3, 1): reduce_ticks(6)}

    def feed_step(k):
        feed(k, table3)
        at_end(k, [2 * i + 1 for i in range(n)])

    each(n, feed_step)
    r_tick(8)
    out_copy = pltpu.make_async_copy(acc, r.layer_out, local_sem.at[14])

    def after_feed(i):
        rows = chunk(i)
        keep = keep_of(i)
        acc[rows] = r.h2[rows] + (acc[rows] + r.bias_out[...].reshape(1, model)) * keep
        down = r.upstream[rows].astype(F32) + norm_backward(r.h2[rows], 2, da[rows])
        dh[rows] = down
        r.e[rows] = (down * keep).astype(BF16)
        da[rows] = zeros
        r.dm[rows] = zeros

    each_chunk(after_feed)
    out_copy.start()
    table4 = {(k, 1): reduce_ticks(9 + 2 * k) for k in range(n)}

    def cross_step(k):
        attend_backward(k, table4, 1, r.a2, r.m)
        at_end(k, [10 + 2 * i for i in range(n)])

    each(n, cross_step)
    memory_copy = pltpu.make_async_copy(r.dm, r.memory_out, local_sem.at[15])
    memory_copy.start()

    def before_cross(i):
        rows = chunk(i)
        down = dh[rows] + norm_backward(r.h1[rows], 1, da[rows])
        dh[rows] = down
        r.e[rows] = (down * keep_of(i)).astype(BF16)
        da[rows] = zeros

    each_chunk(before_cross)
    r_tick(17)
    table5 = {(k, 1): reduce_ticks(18 + 2 * k) for k in range(n)}

    def self_step(k):
        attend_backward(k, table5, 0, r.a1, r.a1)
        at_end(k, [19 + 2 * i for i in range(n)])

    each(n, self_step)

    def before_self(i):
        rows = chunk(i)
        dh[rows] = dh[rows] + norm_backward(x[rows].astype(F32), 0, da[rows])

    each_chunk(before_self)
    grad_copy = pltpu.make_async_copy(dh, r.input_grad, local_sem.at[16])
    grad_copy.start()

    small = SumSmall(place, r.slots, r.small_sems)

    def small_start():
        own = r.slots.at[0]
        own[...] = jnp.zeros(own.shape, F32)
        for i in range(6):
            own[i:i + 1, :model] = jnp.sum(r.norm_sums[i], axis=0, keepdims=True)
        own[6:7, :model] = jnp.sum(r.out_sums[...], axis=0, keepdims=True)
        tokens = lengths[place.tp * sentences]
        for b in range(1, sentences):
            tokens = tokens + lengths[place.tp * sentences + b]
        own[7:8] = jnp.full((1, own.shape[1]), tokens.astype(F32))
        for i in range(n):
            own[8 + i:9 + i] = jnp.sum(r.bias_sums[i], axis=0, keepdims=True)
        small.start()

    add(26, 5, small_start)
    for stage in range(2):
        add(27 + stage, 5, small.exchange, stage)
    final = max(plan)
    for tick in range(26, final + 1):
        r_tick(tick)
    r.small_out[...] = small.total()
    bias.finish()
    for copy in (out_copy, memory_copy, grad_copy):
        copy.wait()
    for g in range(4):
        reduce.finish(g)
        store(g).wait()
    small.finish()


def call(kernel, name, ins, outs, scratch, spaces, **options):
    trees = (ins, outs, scratch)
    structure = jax.tree_util.tree_structure(trees)

    def body(*refs):
        groups = jax.tree_util.tree_unflatten(structure, refs)
        kernel(types.SimpleNamespace(**groups[0], **groups[1], **groups[2]))

    def specs(group):
        return [
            pl.BlockSpec(memory_space=spaces.get(key, pltpu.VMEM))
            for key in sorted(group) for _ in jax.tree_util.tree_leaves(group[key])
        ]

    leaves = jax.tree_util.tree_leaves
    values = pl.pallas_call(
        body,
        out_shape=leaves(outs),
        in_specs=specs(ins),
        out_specs=specs(outs),
        scratch_shapes=leaves(scratch),
        compiler_params=pltpu.CompilerParams(**options),
        name=name,
    )(*leaves(ins))
    return types.SimpleNamespace(**jax.tree_util.tree_unflatten(jax.tree_util.tree_structure(outs), values))


def run_layer(ins):
    n, extra = lax.axis_size("tp"), lax.axis_size("dp") // 2
    owned, model = ins["x_in"].shape
    memory, shards = ins["memory_in"], ins["shards"]
    local, units = shards[1].shape[0], ins["bias_in"].shape[0]
    small = (16, units)
    assert n <= 8 and units >= model and memory.shape[0] >= 3
    shapes = [(n, 4 * local, model)] * 2 + [(n,) + shards[5].shape, (n,) + shards[6].shape]
    small_slots = SumSmall.slots(n, extra)

    def vmem(*shape):
        return pltpu.VMEM(shape, BF16)

    def wide(*shape):
        return pltpu.VMEM(shape, F32)

    def eighths(*lead, parts=1):
        return [vmem(*lead, rows * parts // 8, columns) for _, rows, columns in shapes]

    dma = pltpu.SemaphoreType.DMA
    scratch = dict(
        w=[vmem(*shape) for shape in shapes],
        bias=wide(n, 8, units),
        x=vmem(owned, model),
        memory=vmem(*memory.shape),
        upstream=vmem(owned, model),
        a1=vmem(owned, model),
        m=vmem(owned, model),
        h1=wide(owned, model),
        h2=wide(owned, model),
        acc=wide(owned, model),
        da=wide(owned, model),
        t=[vmem(n, 3 * local, owned)] * 2,
        c=[vmem(n, local, owned)] * 2,
        p=[vmem(n, owned // LEN * (local // HD), LEN, LEN)] * 2,
        dt=vmem(3 * local, owned),
        dc=vmem(local, owned),
        a3t=vmem(model, owned),
        scores=wide(owned // LEN * (local // HD), LEN, LEN),
        ds=vmem(owned // LEN * (local // HD), LEN, LEN),
        before=wide(owned, units),
        down=wide(owned, units),
        hidden=vmem(owned, units),
        dhidden=vmem(owned, units),
        bias_sums=wide(n, 8, units),
        norm_sums=wide(6, 8, model),
        out_sums=wide(8, model),
        half=eighths(n, parts=4),
        plane=eighths(n, parts=3),
        line=eighths(n),
        extra=eighths(extra),
        total=eighths(parts=8),
        slots=wide(small_slots, *small),
        gather_sems=dma((Gather.KINDS, 4, n)),
        bias_sems=dma((3, n)),
        reduce_sems=dma((Reduce.KINDS, 4, max(n, extra))),
        small_sems=dma((2, small_slots)),
        local_sems=dma((17,)),
    )
    rows = jax.ShapeDtypeStruct((owned, model), F32)
    outs = dict(
        layer_out=rows, input_grad=rows, memory_out=rows, small_out=jax.ShapeDtypeStruct(small, F32),
        blocks=[jax.ShapeDtypeStruct(shape[1:], BF16) for shape in shapes],
    )
    smem, hbm = pltpu.SMEM, pl.ANY
    spaces = dict(
        lengths=smem, src_lengths=smem, configs=smem, x_in=hbm, memory_in=hbm, upstream_in=hbm, shards=hbm,
        layer_out=hbm, input_grad=hbm, memory_out=hbm, blocks=hbm,
    )
    return call(
        layer_kernel, "layer", ins, outs, scratch, spaces,
        collective_id=1, has_side_effects=True, vmem_limit_bytes=64 * 2**20,
    )


def finish_kernel(r):
    small, configs, sems = r.small, r.configs, r.sems
    model = r.gain_grad.shape[1]
    layers = r.memory_grad.shape[0]
    place = lax.axis_index("tp")
    local = r.grads[1].shape[0]
    parts = (
        (0, 0, 3 * local), (0, 3 * local, local),
        (1, 0, local), (1, local, 2 * local), (1, 3 * local, local),
        (2, 0, r.block[2].shape[0]), (3, 0, r.block[3].shape[0]),
    )
    loads = [pltpu.make_async_copy(r.blocks[g], r.block[g], sems.at[g]) for g in range(4)]
    rows = [
        pltpu.make_async_copy(source, target, sems.at[4 + i])
        for i, (source, target) in enumerate(((r.layer_in, r.layer), (r.grad_in, r.grad), (r.source_in, r.source)))
    ]
    outs = [pltpu.make_async_copy(r.layer, r.layer_out, sems.at[7]), pltpu.make_async_copy(r.grad, r.input_grad, sems.at[8])]
    for copy in rows + loads:
        copy.start()
    inverse = 1.0 / small[7:8, :1]
    r.gain_grad[...] = small[:3, :model] * inverse
    r.shift_grad[...] = small[3:6, :model] * inverse
    r.bias_out_grad[...] = (small[6:7, :model] * inverse).reshape(model)
    r.bias_in_grad[...] = (small[pl.ds(8 + place, 1)] * inverse).reshape(small.shape[1])
    width, depth = configs[0, 0], configs[0, 3]
    factor = (column(1, (1, model)) < width).astype(F32) / jnp.full((1, 1), depth.astype(F32))
    for i in range(2):
        rows[i].wait()
        outs[i].start()
    rows[2].wait()

    def spread(i):
        part = pl.ds(pl.multiple_of(i * 64, 64), 64)
        value = r.source[part] * factor
        for level in range(layers):
            chosen = (jnp.full((1, 1), depth) >= layers - level).astype(F32)
            r.memories[level, part] = value * chosen

    each(r.source.shape[0] // 64, spread)
    outs.append(pltpu.make_async_copy(r.memories, r.memory_grad, sems.at[9]))
    outs[2].start()
    for i, (g, start, count) in enumerate(parts):
        if start == 0:
            loads[g].wait()

        size = 80 if count % 80 == 0 else 96

        def scale(at):
            there = pl.ds(pl.multiple_of(start + at * size, 16), size)
            r.wide[g][there] = r.block[g][there].astype(F32) * inverse

        each(count // size, scale)
        outs.append(pltpu.make_async_copy(r.wide[g].at[pl.ds(start, count)], r.grads[i], sems.at[10 + i]))
        outs[-1].start()
    for copy in outs:
        copy.wait()


def run_finish(ins, layers):
    blocks, small = ins["blocks"], ins["small"]
    rows = ins["layer_in"].shape
    local, units = blocks[0].shape[0] // 4, small.shape[1]

    def shape(*dims):
        return jax.ShapeDtypeStruct(dims, F32)

    counts = (3 * local, local, local, 2 * local, local)
    outs = dict(
        layer_out=shape(*rows), input_grad=shape(*rows), memory_grad=shape(layers, *rows),
        gain_grad=shape(3, rows[1]), shift_grad=shape(3, rows[1]), bias_in_grad=shape(units), bias_out_grad=shape(rows[1]),
        grads=[shape(count, rows[1]) for count in counts] + [shape(*blocks[2].shape), shape(*blocks[3].shape)],
    )
    scratch = dict(
        layer=pltpu.VMEM(rows, F32), grad=pltpu.VMEM(rows, F32), source=pltpu.VMEM(rows, F32),
        memories=pltpu.VMEM((layers,) + rows, F32),
        block=[pltpu.VMEM(block.shape, BF16) for block in blocks],
        wide=[pltpu.VMEM(block.shape, F32) for block in blocks],
        sems=pltpu.SemaphoreType.DMA((17,)),
    )
    hbm = pl.ANY
    spaces = dict(
        configs=pltpu.SMEM, layer_in=hbm, grad_in=hbm, source_in=hbm, blocks=hbm,
        layer_out=hbm, input_grad=hbm, memory_grad=hbm, grads=hbm,
    )
    return call(finish_kernel, "finish", ins, outs, scratch, spaces, vmem_limit_bytes=60 * 2**20)


def per_device(
    inputs, memory, out_grad, lengths, src_lengths, configs, norm_gain, norm_bias,
    self_qkv, self_out, cross_q, cross_kv, cross_out, ffn_in, ffn_in_bias, ffn_out, ffn_out_bias,
):
    model = inputs.shape[1]
    layers = memory.shape[0]
    local = self_out.shape[0]
    done = run_layer(dict(
        lengths=lengths, src_lengths=src_lengths, configs=configs, gains=norm_gain, shifts=norm_bias,
        bias_in=ffn_in_bias, bias_out=ffn_out_bias, x_in=inputs, memory_in=memory, upstream_in=out_grad,
        shards=[
            self_qkv.transpose(1, 2, 0).reshape(3 * local, model), self_out, cross_q.T,
            cross_kv.transpose(1, 2, 0).reshape(2 * local, model), cross_out, ffn_in, ffn_out,
        ],
    ))
    out = run_finish(dict(
        configs=configs, small=done.small_out, layer_in=done.layer_out, grad_in=done.input_grad,
        source_in=done.memory_out, blocks=done.blocks,
    ), layers)
    grads = out.grads
    return (
        out.layer_out,
        out.input_grad,
        out.memory_grad,
        out.gain_grad,
        out.shift_grad,
        grads[0].reshape(3, local, model).transpose(2, 0, 1),
        grads[1],
        grads[2].T,
        grads[3].reshape(2, local, model).transpose(2, 0, 1),
        grads[4],
        grads[5],
        out.bias_in_grad,
        grads[6],
        out.bias_out_grad,
    )


def solution(mesh):
    rows = P(("grp", "dp", "tp"), None)
    stack = P(None, ("grp", "dp", "tp"), None)
    weights = (
        P(None, None, "tp"), P("tp", None), P(None, "tp"), P(None, None, "tp"), P("tp", None),
        P(None, "tp"), P("tp"), P("tp", None), P(),
    )
    return jax.shard_map(
        per_device,
        mesh=mesh,
        in_specs=(rows, stack, rows, P(("grp", "dp")), P(("grp", "dp")), P("grp", None), P(), P()) + weights,
        out_specs=(rows, rows, stack, P(), P()) + weights,
        check_vma=False,
    )
```

profile of v0, /device:TPU:1, one launch (start us, length us, event | category | flops | bytes accessed | tf_op | source)
XLA Modules:
  0.0 192.0 jit_solution(6262189431256587692)
XLA Ops:
  0.7 182.7 %layer.1 = (bf16[640,640]{1,0:T(8,128)(2,1)}, bf16[640,640]{1,0:T(8,128)(2,1)}, bf16[640,768]{1,0:T(8,128)(2,1)}, bf16[768,640]{1,0:T(8,128)(2,1)}, f32[512,640]...) custom-call(f32[768]{0:T(1024)} %refs_0_.1, f32[640]{0:T(1024)} %refs_1_.1, ...), custom_call_target="tpu_custom_call" | custom-call | tf_op jit(solution)/shard_map/layer/pallas_call | solution.py:851
  183.4 8.4 %finish.1 = (f32[768]{0:T(1024)}, f32[640]{0:T(1024)}, f32[3,640]{1,0:T(4,128)}, f32[480,640]{1,0:T(8,128)}, f32[160,640]{1,0:T(8,128)}, /*index=5*/f32[160,640]...) custom-call(bf16[640,640]{1,0:T(8,128)(2,1)} %get-tuple-element.36.r, ...), custom_call_target="tpu_custom_call" | custom-call | tf_op jit(solution)/shard_map/finish/pallas_call | solution.py:851
where the time goes:
time: 192 us
  Pallas kernels  191 us (99%)
    pallas_call x2, Pallas kernels, call(): pl.pallas_call(body, out_shape=leaves(outs), in_specs=specs(ins), out_spe...  191 us

commit v1 on v0

--- a/solution.py
+++ b/solution.py
@@ -563,6 +563,7 @@
         w, t, c, p = weights[g], r.t[g], r.c[g], r.p[g]
         j = block_last(k)
         e, dt, dc = r.e, r.dt, r.dc
+        gather.drain(g, j)
         dc_all = dot_nt(w[j, 3 * local:], e[...])
         for h in range(heads_here):
             dc[h * HD:(h + 1) * HD] = (dc_all[h * HD:(h + 1) * HD] * head_keep(j, h)).astype(BF16)
@@ -570,6 +571,9 @@
         dc_of = [dc[h * HD:(h + 1) * HD, lanes(b)] for b, h in pairs]
         for i, (_, _, values) in enumerate(heads_of):
             r.scores[i] = dot_tn(values, dc_of[i])
+        for i, (b, h) in enumerate(pairs):
+            dt[bands(h)[2], lanes(b)] = dot_nt(dc_of[i], p[j, i]).astype(BF16)
+        w[j, 3 * local:] = dot_nn(c[j], e[...]).astype(BF16)
         for i, b, h, start in quarters:
             part, size = pl.ds(start, 128), reach(g, start)
             dp, wide = r.scores[i, :size, part], p[j, i, :size, part].astype(F32)
@@ -577,12 +581,10 @@
             if size < LEN:
                 r.ds[i, size:, part] = jnp.zeros((LEN - size, 128), BF16)
         for i, (b, h) in enumerate(pairs):
-            (query, keys, _), (dq, dk, dv) = heads_of[i], bands(h)
-            dt[dv, lanes(b)] = dot_nt(dc_of[i], p[j, i]).astype(BF16)
+            (query, keys, _), (dq, dk, _) = heads_of[i], bands(h)
             dt[dq, lanes(b)] = (dot_nn(keys, r.ds[i]) * SCALE).astype(BF16)
             dt[dk, lanes(b)] = (dot_nt(query, r.ds[i]) * SCALE).astype(BF16)
         hooks(table, k, 1)
-        gather.drain(g, j)
         if g == 0:
             da[...] = da[...] + dot_tn(dt[...], w[j, :3 * local])
             w[j, :3 * local] = dot_nn(dt[...], query_rows[...]).astype(BF16)
@@ -591,40 +593,33 @@
             r.dm[...] = r.dm[...] + dot_tn(dt[local:], w[j, local:3 * local])
             w[j, :local] = dot_nn(dt[:local], query_rows[...]).astype(BF16)
             w[j, local:3 * local] = dot_nn(dt[local:], key_rows[...]).astype(BF16)
-        w[j, 3 * local:] = dot_nn(c[j], e[...]).astype(BF16)
 
     def feed(k, table):
         j = block(k)
         w_up, w_down = weights[2], weights[3]
         hooks(table, k, 0)
-        r.before[...] = dot_nn(r.a3[...], w_up[j]) + r.bias[j, 0:1]
-        r.down[...] = dot_nt(r.e[...], w_down[j])
-        step_lanes = units // 2
-
-        def bend(i):
-            for start in range(0, units, step_lanes):
-                part = pl.ds(start, step_lanes)
-                unit = column(1, (1, step_lanes)) + (j * units + start)
-                kept = jnp.where(unit < hidden_units, 0.5, 0.0)
-                sums = r.bias_sums[j, :, part]
-                for line in range(4):
-                    rows = pl.ds(pl.multiple_of(i * 64, 64) + line * 16, 16)
-                    before = r.before[rows, part]
-                    square = before * before
-                    bent = jnp.tanh(before * (ROOT + ROOT * CUBE * square))
-                    half = kept + kept * bent
-                    through = before * half
-                    r.hidden[rows, part] = through.astype(BF16)
-                    slope = half + (through - through * bent) * (ROOT + 3.0 * CUBE * ROOT * square)
-                    du = (r.down[rows, part] * slope).astype(BF16)
-                    r.dhidden[rows, part] = du
-                    sums = sums + fold(du.astype(F32))
-                r.bias_sums[j, :, part] = sums
-
-        each(owned // 64, bend)
+        unit = column(1, (1, units)) + j * units
+        kept = jnp.where(unit < hidden_units, 0.5, 0.0)
+        found = []
+        for b in range(sentences):
+            rows = sentence(b)
+            found.append((dot_nn(r.a3[rows], w_up[j]) + r.bias[j, 0:1], dot_nt(r.e[rows], w_down[j])))
+        for b, (before, down) in enumerate(found):
+            rows = sentence(b)
+            square = before * before
+            bent = jnp.tanh(before * (ROOT + ROOT * CUBE * square))
+            half = kept + kept * bent
+            through = before * half
+            r.hidden[rows] = through.astype(BF16)
+            slope = half + (through - through * bent) * (ROOT + 3.0 * CUBE * ROOT * square)
+            du = (down * slope).astype(BF16)
+            r.dhidden[rows] = du
+            r.bias_sums[j] = r.bias_sums[j] + fold(du.astype(F32))
+        for b in range(sentences):
+            rows = sentence(b)
+            acc[rows] = acc[rows] + dot_nn(r.hidden[rows], w_down[j])
+            da[rows] = da[rows] + dot_nt(r.dhidden[rows], w_up[j])
         hooks(table, k, 1)
-        acc[...] = acc[...] + dot_nn(r.hidden[...], w_down[j])
-        da[...] = da[...] + dot_nt(r.dhidden[...], w_up[j])
         gather.drain(2, j)
         gather.drain(3, j)
         w_down[j] = dot_tn(r.hidden[...], r.e[...]).astype(BF16)

time: 192 us -> 188 us (0.979)
  Pallas kernels: 191 us -> 187 us
    pallas_call x2, Pallas kernels: 191 us -> 187 us  [call(): pl.pallas_call(body, out_shape=leaves(outs), in_specs=specs(ins), out_spe...]
where the time goes in v1:
time: 188 us
  Pallas kernels  187 us (99%)
    pallas_call x2, Pallas kernels, call(): pl.pallas_call(body, out_shape=leaves(outs), in_specs=specs(ins), out_spe...  187 us

profile of v1, /device:TPU:1, one launch (start us, length us, event | category | flops | bytes accessed | tf_op | source)
XLA Modules:
  0.0 187.7 jit_solution(7695694500768350342)
XLA Ops:
  0.7 178.4 %layer.1 = (bf16[640,640]{1,0:T(8,128)(2,1)}, bf16[640,640]{1,0:T(8,128)(2,1)}, bf16[640,768]{1,0:T(8,128)(2,1)}, bf16[768,640]{1,0:T(8,128)(2,1)}, f32[512,640]...) custom-call(f32[768]{0:T(1024)} %refs_0_.1, f32[640]{0:T(1024)} %refs_1_.1, ...), custom_call_target="tpu_custom_call" | custom-call | tf_op jit(solution)/shard_map/layer/pallas_call | solution.py:846
  179.1 8.4 %finish.1 = (f32[768]{0:T(1024)}, f32[640]{0:T(1024)}, f32[3,640]{1,0:T(4,128)}, f32[480,640]{1,0:T(8,128)}, f32[160,640]{1,0:T(8,128)}, /*index=5*/f32[160,640]...) custom-call(bf16[640,640]{1,0:T(8,128)(2,1)} %get-tuple-element.36.r, ...), custom_call_target="tpu_custom_call" | custom-call | tf_op jit(solution)/shard_map/finish/pallas_call | solution.py:846

commit v2 on v1

--- a/solution.py
+++ b/solution.py
@@ -446,10 +446,19 @@
             bias.start()
     order = [(g, k) for g in (0, 1) for k in range(n - 1)] + [(g, k) for k in range(n - 1) for g in (2, 3)]
 
-    def g_tick(tick):
-        for stage in range(4):
-            if 0 <= tick - stage < len(order):
-                gather.step(*order[tick - stage], stage)
+    places = (
+        (0, 1, 2, 5), (1, 2, 4, 7), (2, 3, 6, 9), (3, 5, 7, 11), (4, 6, 9, 12), (6, 8, 10, 11),
+        (7, 10, 11, 15), (9, 11, 13, 15), (11, 12, 15, 18), (12, 15, 20, 23), (13, 16, 21, 23), (15, 18, 22, 25),
+    )
+    assert len(places) == len(order)
+
+    def gather_at(spot):
+        found = [(stage, e) for e, stages in enumerate(places) for stage, at in enumerate(stages) if at == spot]
+        for stage, e in sorted(found):
+            gather.step(*order[e], stage)
+
+    def gather_table(start):
+        return {(k, b): [functools.partial(gather_at, start + 2 * k + b)] for k in range(n) for b in range(2)}
 
     def block(k):
         later = (k + n - 1) // n
@@ -532,8 +541,6 @@
         return pl.ds(b * LEN, LEN)
 
     pairs = [(b, h) for b in range(sentences) for h in range(heads_here)]
-
-    quarters = [(i, b, h, start) for i, (b, h) in enumerate(pairs) for start in range(0, LEN, 128)]
 
     def attend(k, table, g, allowed):
         w, t, c, p = weights[g], r.t[g], r.c[g], r.p[g]
@@ -547,14 +554,14 @@
         heads_of = [[t[j, band, lanes(b)] for band in bands(h)] for b, h in pairs]
         for i, (query, keys, _) in enumerate(heads_of):
             r.scores[i] = dot_tn(keys, query)
-        for i, b, h, start in quarters:
-            part, size = pl.ds(start, 128), reach(g, start)
-            score = jnp.where(allowed(b, start, size), r.scores[i, :size, part], NEGATIVE)
-            raised = jnp.exp2((score - jnp.max(score, axis=0, keepdims=True)) * (SCALE * LOG2E))
-            p[j, i, :size, part] = (raised * (1.0 / jnp.sum(raised, axis=0, keepdims=True))).astype(BF16)
-            if size < LEN:
-                p[j, i, size:, part] = jnp.zeros((LEN - size, 128), BF16)
         for i, (b, h) in enumerate(pairs):
+            for start in range(0, LEN, 128):
+                part, size = pl.ds(start, 128), reach(g, start)
+                score = jnp.where(allowed(b, start, size), r.scores[i, :size, part], NEGATIVE)
+                raised = jnp.exp2((score - jnp.max(score, axis=0, keepdims=True)) * (SCALE * LOG2E))
+                p[j, i, :size, part] = (raised * (1.0 / jnp.sum(raised, axis=0, keepdims=True))).astype(BF16)
+                if size < LEN:
+                    p[j, i, size:, part] = jnp.zeros((LEN - size, 128), BF16)
             c[j, pl.ds(h * HD, HD), lanes(b)] = (dot_nn(heads_of[i][2], p[j, i]) * head_keep(j, h)).astype(BF16)
         hooks(table, k, 1)
         acc[...] = acc[...] + dot_tn(c[j], w[j, 3 * local:])
@@ -574,14 +581,14 @@
         for i, (b, h) in enumerate(pairs):
             dt[bands(h)[2], lanes(b)] = dot_nt(dc_of[i], p[j, i]).astype(BF16)
         w[j, 3 * local:] = dot_nn(c[j], e[...]).astype(BF16)
-        for i, b, h, start in quarters:
-            part, size = pl.ds(start, 128), reach(g, start)
-            dp, wide = r.scores[i, :size, part], p[j, i, :size, part].astype(F32)
-            r.ds[i, :size, part] = (wide * (dp - jnp.sum(dp * wide, axis=0, keepdims=True))).astype(BF16)
-            if size < LEN:
-                r.ds[i, size:, part] = jnp.zeros((LEN - size, 128), BF16)
         for i, (b, h) in enumerate(pairs):
             (query, keys, _), (dq, dk, _) = heads_of[i], bands(h)
+            for start in range(0, LEN, 128):
+                part, size = pl.ds(start, 128), reach(g, start)
+                dp, wide = r.scores[i, :size, part], p[j, i, :size, part].astype(F32)
+                r.ds[i, :size, part] = (wide * (dp - jnp.sum(dp * wide, axis=0, keepdims=True))).astype(BF16)
+                if size < LEN:
+                    r.ds[i, size:, part] = jnp.zeros((LEN - size, 128), BF16)
             dt[dq, lanes(b)] = (dot_nn(keys, r.ds[i]) * SCALE).astype(BF16)
             dt[dk, lanes(b)] = (dot_nt(query, r.ds[i]) * SCALE).astype(BF16)
         hooks(table, k, 1)
@@ -634,7 +641,7 @@
         da[rows] = zeros
 
     each_chunk(begin)
-    g_tick(0)
+    gather_at(0)
     loads[1].wait()
 
     def mix(i):
@@ -646,7 +653,7 @@
         r.m[rows] = (total * inv_depth * width_mask).astype(BF16)
 
     each_chunk(mix)
-    g_tick(1)
+    gather_at(1)
     loads[2].wait()
     r.out_sums[...] = jnp.zeros(r.out_sums.shape, F32)
 
@@ -657,22 +664,13 @@
         r.e[rows] = masked.astype(BF16)
 
     each_chunk(grad_in)
-    g_tick(2)
-
-    def ticks(*numbers):
-        return [functools.partial(g_tick, i) for i in numbers]
+    gather_at(2)
 
     others = n - 1
     assert n == 4
-    table = {
-        (0, 1): ticks(3),
-        (1, 0): ticks(4) + [functools.partial(bias.step, 0)],
-        (1, 1): ticks(5),
-        (2, 0): [functools.partial(bias.step, 1)],
-        (2, 1): ticks(6),
-        (3, 0): [functools.partial(bias.step, 2)],
-        (3, 1): ticks(7),
-    }
+    table = gather_table(3)
+    for k in range(others):
+        table[k + 1, 0].append(functools.partial(bias.step, k))
     each(n, lambda k: attend(k, table, 0, causal))
 
     def after_self(i):
@@ -683,7 +681,7 @@
         acc[rows] = zeros
 
     each_chunk(after_self)
-    table2 = {(0, 0): ticks(8), (0, 1): ticks(9), (1, 1): ticks(10), (2, 1): ticks(11), (3, 1): ticks(12)}
+    table2 = gather_table(11)
     each(n, lambda k: attend(k, table2, 1, crossing))
 
     def after_cross(i):
@@ -712,9 +710,9 @@
         return pltpu.make_async_copy(r.total[g], r.blocks[g], local_sem.at[10 + g])
 
     times = {
-        3: ([(1, 2, 6, 10), (3, 4, 8, 11), (5, 6, 9, 13), (7, 9, 11, 15)], (17, 19, 21, 23)),
-        2: ([(1, 3, 6, 9), (3, 6, 8, 11), (5, 8, 10, 13), (7, 9, 12, 16)], (18, 20, 22, 24)),
-        1: ([(10, 11, 14, 16), (12, 14, 16, 18), (14, 15, 19, 21), (16, 17, 19, 21)], (23, 25, 27, 29)),
+        3: ([(1, 2, 6, 10), (3, 4, 8, 11), (5, 6, 9, 13), (7, 9, 11, 15)], (17, 19, 21, 25)),
+        2: ([(1, 3, 6, 9), (3, 6, 8, 11), (5, 8, 10, 13), (7, 9, 12, 16)], (19, 21, 23, 26)),
+        1: ([(10, 11, 14, 16), (12, 14, 16, 18), (14, 15, 19, 21), (16, 17, 19, 21)], (24, 27, 28, 29)),
         0: ([(19, 20, 22, 24), (21, 22, 24, 25), (23, 24, 25, 26), (25, 26, 27, 28)], (28, 29, 30, 31)),
     }
     for late, g in enumerate((3, 2, 1, 0)):
@@ -739,7 +737,9 @@
             def _():
                 r_tick(number)
 
-    table3 = {(0, 0): ticks(13), (0, 1): ticks(14), (1, 1): reduce_ticks(2), (2, 1): reduce_ticks(4), (3, 1): reduce_ticks(6)}
+    table3 = gather_table(19)
+    for k in range(1, n):
+        table3[k, 1] += reduce_ticks(2 * k)
 
     def feed_step(k):
         feed(k, table3)

time: 188 us -> 185 us (0.984)
  Pallas kernels: 187 us -> 184 us
    pallas_call x2, Pallas kernels: 187 us -> 184 us  [call(): pl.pallas_call(body, out_shape=leaves(outs), in_specs=specs(ins), out_spe...]
where the time goes in v2:
time: 185 us
  Pallas kernels  184 us (99%)
    pallas_call x2, Pallas kernels, call(): pl.pallas_call(body, out_shape=leaves(outs), in_specs=specs(ins), out_spe...  184 us

profile of v2, /device:TPU:1, one launch (start us, length us, event | category | flops | bytes accessed | tf_op | source)
XLA Modules:
  0.0 185.1 jit_solution(12002696792216594373)
XLA Ops:
  0.7 175.9 %layer.1 = (bf16[640,640]{1,0:T(8,128)(2,1)}, bf16[640,640]{1,0:T(8,128)(2,1)}, bf16[640,768]{1,0:T(8,128)(2,1)}, bf16[768,640]{1,0:T(8,128)(2,1)}, f32[512,640]...) custom-call(f32[768]{0:T(1024)} %refs_0_.1, f32[640]{0:T(1024)} %refs_1_.1, ...), custom_call_target="tpu_custom_call" | custom-call | tf_op jit(solution)/shard_map/layer/pallas_call | solution.py:846
  176.5 8.4 %finish.1 = (f32[768]{0:T(1024)}, f32[640]{0:T(1024)}, f32[3,640]{1,0:T(4,128)}, f32[480,640]{1,0:T(8,128)}, f32[160,640]{1,0:T(8,128)}, /*index=5*/f32[160,640]...) custom-call(bf16[640,640]{1,0:T(8,128)(2,1)} %get-tuple-element.36.r, ...), custom_call_target="tpu_custom_call" | custom-call | tf_op jit(solution)/shard_map/finish/pallas_call | solution.py:846

commit v3 on v2

--- a/solution.py
+++ b/solution.py
@@ -466,7 +466,7 @@
 
     def block_last(k):
         own = k // (n - 1)
-        return own * place.tp + (1 - own) * place.nth_block(k)
+        return own * place.tp + (1 - own) * place.nth_block((n - 2 - k) * (1 - own))
 
     def hooks(table, k, b):
         for (kk, bb), steps in table.items():
@@ -622,8 +622,6 @@
             du = (down * slope).astype(BF16)
             r.dhidden[rows] = du
             r.bias_sums[j] = r.bias_sums[j] + fold(du.astype(F32))
-        for b in range(sentences):
-            rows = sentence(b)
             acc[rows] = acc[rows] + dot_nn(r.hidden[rows], w_down[j])
             da[rows] = da[rows] + dot_nt(r.dhidden[rows], w_up[j])
         hooks(table, k, 1)

time: 185 us -> 188 us (1.016)
  Pallas kernels: 184 us -> 186 us
    pallas_call x2, Pallas kernels: 184 us -> 186 us  [call(): pl.pallas_call(body, out_shape=leaves(outs), in_specs=specs(ins), out_spe...]
where the time goes in v3:
time: 188 us; the launch traced here: 187 us
  Pallas kernels  186 us (99%)
    pallas_call x2, Pallas kernels, call(): pl.pallas_call(body, out_shape=leaves(outs), in_specs=specs(ins), out_spe...  186 us

profile of v3, /device:TPU:1, one launch (start us, length us, event | category | flops | bytes accessed | tf_op | source)
XLA Modules:
  0.0 187.3 jit_solution(12191834780072694667)
XLA Ops:
  0.7 178.1 %layer.1 = (bf16[640,640]{1,0:T(8,128)(2,1)}, bf16[640,640]{1,0:T(8,128)(2,1)}, bf16[640,768]{1,0:T(8,128)(2,1)}, bf16[768,640]{1,0:T(8,128)(2,1)}, f32[512,640]...) custom-call(f32[768]{0:T(1024)} %refs_0_.1, f32[640]{0:T(1024)} %refs_1_.1, ...), custom_call_target="tpu_custom_call" | custom-call | tf_op jit(solution)/shard_map/layer/pallas_call | solution.py:844
  178.7 8.4 %finish.1 = (f32[768]{0:T(1024)}, f32[640]{0:T(1024)}, f32[3,640]{1,0:T(4,128)}, f32[480,640]{1,0:T(8,128)}, f32[160,640]{1,0:T(8,128)}, /*index=5*/f32[160,640]...) custom-call(bf16[640,640]{1,0:T(8,128)(2,1)} %get-tuple-element.36.r, ...), custom_call_target="tpu_custom_call" | custom-call | tf_op jit(solution)/shard_map/finish/pallas_call | solution.py:844

commit v4 on v2

--- a/solution.py
+++ b/solution.py
@@ -146,13 +146,26 @@
         for needed, copy in self.relays(g, self.place.tp):
             pl.when(needed)(copy.start)
 
-    def step(self, g, k, stage):
+    def passes(self, j):
+        p = self.place
+        up = jnp.logical_and(j < p.tp, p.has_above)
+        down = jnp.logical_and(j > p.tp, p.has_below)
+        return jnp.logical_or(up, down)
+
+    def relay(self, g, k):
         j = self.place.nth_block(k)
-        if stage == 0:
+
+        @pl.when(self.passes(j))
+        def _():
             relays = self.relays(g, j)
             relays[0][1].wait_recv()
             for needed, copy in relays:
                 pl.when(needed)(copy.start)
+
+    def step(self, g, k, stage):
+        j = self.place.nth_block(k)
+        if stage == 0:
+            pl.when(jnp.logical_not(self.passes(j)))(self.relays(g, j)[0][1].wait_recv)
         self.spread(g, j).step(stage)
 
     def drain(self, g, j):
@@ -455,7 +468,11 @@
     def gather_at(spot):
         found = [(stage, e) for e, stages in enumerate(places) for stage, at in enumerate(stages) if at == spot]
         for stage, e in sorted(found):
+            if stage == 0 and e == 0:
+                gather.relay(*order[0])
             gather.step(*order[e], stage)
+            if stage == 0 and e + 1 < len(order):
+                gather.relay(*order[e + 1])
 
     def gather_table(start):
         return {(k, b): [functools.partial(gather_at, start + 2 * k + b)] for k in range(n) for b in range(2)}

time: 185 us -> 188 us (1.016)
  Pallas kernels: 184 us -> 186 us
    pallas_call x2, Pallas kernels: 184 us -> 186 us  [call(): pl.pallas_call(body, out_shape=leaves(outs), in_specs=specs(ins), out_spe...]
where the time goes in v4:
time: 188 us; the launch traced here: 187 us
  Pallas kernels  186 us (99%)
    pallas_call x2, Pallas kernels, call(): pl.pallas_call(body, out_shape=leaves(outs), in_specs=specs(ins), out_spe...  186 us

profile of v4, /device:TPU:1, one launch (start us, length us, event | category | flops | bytes accessed | tf_op | source)
XLA Modules:
  0.0 187.3 jit_solution(7973483160930174171)
XLA Ops:
  0.7 178.0 %layer.1 = (bf16[640,640]{1,0:T(8,128)(2,1)}, bf16[640,640]{1,0:T(8,128)(2,1)}, bf16[640,768]{1,0:T(8,128)(2,1)}, bf16[768,640]{1,0:T(8,128)(2,1)}, f32[512,640]...) custom-call(f32[768]{0:T(1024)} %refs_0_.1, f32[640]{0:T(1024)} %refs_1_.1, ...), custom_call_target="tpu_custom_call" | custom-call | tf_op jit(solution)/shard_map/layer/pallas_call | solution.py:863
  178.7 8.4 %finish.1 = (f32[768]{0:T(1024)}, f32[640]{0:T(1024)}, f32[3,640]{1,0:T(4,128)}, f32[480,640]{1,0:T(8,128)}, f32[160,640]{1,0:T(8,128)}, /*index=5*/f32[160,640]...) custom-call(bf16[640,640]{1,0:T(8,128)(2,1)} %get-tuple-element.36.r, ...), custom_call_target="tpu_custom_call" | custom-call | tf_op jit(solution)/shard_map/finish/pallas_call | solution.py:863

commit v5 on v3

--- a/solution.py
+++ b/solution.py
@@ -466,7 +466,7 @@
 
     def block_last(k):
         own = k // (n - 1)
-        return own * place.tp + (1 - own) * place.nth_block((n - 2 - k) * (1 - own))
+        return own * place.tp + (1 - own) * place.nth_block(k)
 
     def hooks(table, k, b):
         for (kk, bb), steps in table.items():

time: 188 us -> 185 us (0.984)
  Pallas kernels: 186 us -> 184 us
    pallas_call x2, Pallas kernels: 186 us -> 184 us  [call(): pl.pallas_call(body, out_shape=leaves(outs), in_specs=specs(ins), out_spe...]
where the time goes in v5:
time: 185 us
  Pallas kernels  184 us (99%)
    pallas_call x2, Pallas kernels, call(): pl.pallas_call(body, out_shape=leaves(outs), in_specs=specs(ins), out_spe...  184 us

profile of v5, /device:TPU:1, one launch (start us, length us, event | category | flops | bytes accessed | tf_op | source)
XLA Modules:
  0.0 185.1 jit_solution(12002696792216594373)
XLA Ops:
  0.7 175.9 %layer.1 = (bf16[640,640]{1,0:T(8,128)(2,1)}, bf16[640,640]{1,0:T(8,128)(2,1)}, bf16[640,768]{1,0:T(8,128)(2,1)}, bf16[768,640]{1,0:T(8,128)(2,1)}, f32[512,640]...) custom-call(f32[768]{0:T(1024)} %refs_0_.1, f32[640]{0:T(1024)} %refs_1_.1, ...), custom_call_target="tpu_custom_call" | custom-call | tf_op jit(solution)/shard_map/layer/pallas_call | solution.py:844
  176.5 8.4 %finish.1 = (f32[768]{0:T(1024)}, f32[640]{0:T(1024)}, f32[3,640]{1,0:T(4,128)}, f32[480,640]{1,0:T(8,128)}, f32[160,640]{1,0:T(8,128)}, /*index=5*/f32[160,640]...) custom-call(bf16[640,640]{1,0:T(8,128)(2,1)} %get-tuple-element.36.r, ...), custom_call_target="tpu_custom_call" | custom-call | tf_op jit(solution)/shard_map/finish/pallas_call | solution.py:844
